TPU v7x, 32 devices: a whole 2x2x4 slice. The times are simulated.
32 devices in a mesh: det: 4 (over z), tm: 8 (over y, x, core).
Axes of the slice: x: 2, y: 2, z: 4, core: 2. Of those that a mesh axis runs over, the one named last changes fastest.
Arguments:
- iterate: float32 [16, 262144], P(None, ('det', 'tm')), may hold values from -6 to 6
- residual: float32 [16, 262144], P(None, ('det', 'tm')), may hold values from -40 to 40
- direction: float32 [16, 262144], P(None, ('det', 'tm')), may hold values from -2.5 to 2.5
- precond: float32 [262144], P(('det', 'tm')), may hold values from 0.02 to 0.12
- patch_ids: int32 [128, 64], P('det', 'tm'), may hold values from 0 to 4095, as said below
- pixel_in: int32 [128, 8192], P('det', 'tm'), may hold values from 0 to 63
- weights: float32 [128, 8192], P('det', 'tm'), may hold values from 0.5 to 1.5
- filter_diag: float32 [128], P('det'), may hold values from 1 to 1.5
- filter_band: float32 [128, 64], P('det'), may hold values from 0.003125 to 0.0075
Outputs:
- new_iterate: float32 [16, 262144], P(None, ('det', 'tm'))
- new_residual: float32 [16, 262144], P(None, ('det', 'tm'))
- new_direction: float32 [16, 262144], P(None, ('det', 'tm'))
Inputs may be any that keep to these rules, and one draw needn't show every extreme that they name: `patch_ids`: the blocks of one device (detectors 32 d0 .. and time blocks 8 t0 .. of its det index a and tm index c) name, for every owner o = a2 * 8 + c2, exactly 8 patches p with p // 128 = o.
All inputs are finite; a program needn't handle non-finite values.
Results may differ from a plain program's by a relative error of at most 0.0003.
Values sent between devices are 32-bit elements; how exact they have to be, the bound alone decides.
A program may use at most 64 MiB of HBM per device.

v0:
```python
import jax
import jax.numpy as jnp
from jax import lax
from jax.sharding import PartitionSpec as P

PX = 64


def with_halo(cells, sides, width):
    for axis, dim in sides:
        count = lax.axis_size(axis)
        ends = count - 1
        head = lax.slice_in_dim(cells, 0, width, axis=dim)
        tail = lax.slice_in_dim(cells, cells.shape[dim] - width, cells.shape[dim], axis=dim)
        cells = jnp.concatenate(
            [
                lax.ppermute(tail, axis, [(i, (i + 1) % count) for i in range(ends)]),
                cells,
                lax.ppermute(head, axis, [((i + 1) % count, i) for i in range(ends)]),
            ],
            axis=dim,
        )
    return cells


def per_device(
    iterate, residual, direction, precond, patch_ids, pixel_in, weights, filter_diag, filter_band
):
    probes = iterate.shape[0]
    det_rows, time_blocks = patch_ids.shape
    samples = pixel_in.shape[1]
    block_len = samples // time_blocks
    half_band = filter_band.shape[1]
    groups = lax.axis_size("det")
    spans = lax.axis_size("tm")
    devices = groups * spans
    blocks = det_rows * time_blocks
    per_owner = blocks // devices
    own_patches = iterate.shape[1] // PX
    width = probes * PX
    local_old = jnp.sum(residual * precond * residual, axis=1)
    norm_old = lax.psum(local_old, ("det", "tm"))
    patch_flat = patch_ids.reshape(blocks)
    owners = patch_flat // own_patches
    sort_order = jnp.argsort(owners, stable=True)
    inverse = jnp.argsort(sort_order, stable=True)
    requests = (patch_flat[sort_order] % own_patches).reshape(devices, per_owner)
    asked_rows = lax.all_to_all(requests, ("det", "tm"), split_axis=0, concat_axis=0, tiled=True)
    asked_hot = (
        asked_rows.reshape(-1)[:, None] == jnp.arange(own_patches, dtype=jnp.int32)[None, :]
    ).astype(jnp.float32)
    patch_table = (
        direction.reshape(probes, own_patches, PX).transpose(1, 0, 2).reshape(own_patches, width)
    )
    served = jnp.dot(asked_hot, patch_table, precision=lax.Precision.HIGHEST).reshape(
        devices, per_owner, width
    )
    fetched = lax.all_to_all(served, ("det", "tm"), split_axis=0, concat_axis=0, tiled=True)
    block_vals = fetched.reshape(blocks, width)[inverse].reshape(blocks, probes, PX)
    pixel_hot = (
        pixel_in.reshape(blocks, block_len)[:, :, None]
        == jnp.arange(PX, dtype=jnp.int32)[None, None, :]
    ).astype(jnp.float32)
    sample_gain = weights.reshape(blocks, block_len)
    timeline = (
        jnp.einsum("bpx,bsx->bps", block_vals, pixel_hot, precision=lax.Precision.HIGHEST)
        * sample_gain[:, None, :]
    )
    timeline = (
        timeline.reshape(det_rows, time_blocks, probes, block_len)
        .transpose(2, 0, 1, 3)
        .reshape(probes, det_rows, samples)
    )
    padded = with_halo(timeline, (("tm", 2),), half_band)
    windows = jnp.concatenate(
        [
            padded[:, :, :samples].reshape(probes, det_rows, time_blocks, block_len),
            padded[:, :, block_len : samples + block_len].reshape(
                probes, det_rows, time_blocks, block_len
            ),
        ],
        axis=3,
    )
    coeffs = jnp.concatenate([filter_diag[:, None], filter_band], axis=1)
    offsets = jnp.abs(
        jnp.arange(2 * block_len, dtype=jnp.int32)[:, None]
        - jnp.arange(block_len, dtype=jnp.int32)[None, :]
        - half_band
    )
    band_hot = (
        offsets[:, :, None] == jnp.arange(half_band + 1, dtype=jnp.int32)[None, None, :]
    ).astype(jnp.float32)
    toeplitz = jnp.einsum("usk,dk->dus", band_hot, coeffs, precision=lax.Precision.HIGHEST)
    filtered = jnp.einsum("pdju,dus->pdjs", windows, toeplitz, precision=lax.Precision.HIGHEST)
    weighted = (
        filtered.transpose(1, 2, 0, 3).reshape(blocks, probes, block_len) * sample_gain[:, None, :]
    )
    partial_value = jnp.einsum(
        "bps,bsx->bpx", weighted, pixel_hot, precision=lax.Precision.HIGHEST
    ).reshape(blocks, width)
    partial_value = partial_value[sort_order].reshape(devices, per_owner, width)
    collected = lax.all_to_all(
        partial_value, ("det", "tm"), split_axis=0, concat_axis=0, tiled=True
    )
    collected = collected.reshape(devices * per_owner, width)
    summed = lax.dot_general(
        asked_hot, collected, (((0,), (0,)), ((), ())), precision=lax.Precision.HIGHEST
    )
    image_map = (
        summed.reshape(own_patches, probes, PX).transpose(1, 0, 2).reshape(probes, own_patches * PX)
    )
    local_curv = jnp.sum(direction * image_map, axis=1)
    curvature = lax.psum(local_curv, ("det", "tm"))
    step_size = norm_old / curvature
    new_iterate = iterate + step_size[:, None] * direction
    new_residual = residual - step_size[:, None] * image_map
    scaled = precond * new_residual
    norm_new = lax.psum(jnp.sum(new_residual * scaled, axis=1), ("det", "tm"))
    new_direction = scaled + (norm_new / norm_old)[:, None] * direction
    return (new_iterate, new_residual, new_direction)


def solution(mesh):
    in_specs = (
        P(None, ("det", "tm")),
        P(None, ("det", "tm")),
        P(None, ("det", "tm")),
        P(("det", "tm")),
        P("det", "tm"),
        P("det", "tm"),
        P("det", "tm"),
        P("det"),
        P("det", None),
    )
    out_specs = (P(None, ("det", "tm")), P(None, ("det", "tm")), P(None, ("det", "tm")))
    return jax.shard_map(
        per_device, mesh=mesh, in_specs=in_specs, out_specs=out_specs, check_vma=False
    )
```

profile of v0, /device:TPU:0, one launch (start us, length us, event | category | flops | bytes accessed | tf_op | source)
XLA Modules:
  0.0 209.9 jit_solution(2585544996662870150)
XLA Ops:
  0.6 0.8 copy.28
  1.5 3.2 %sort.31 = (s32[256]{0:T(256)}, s32[256]{0:T(256)S(1)}) sort(s32[256]{0:T(256)S(1)} %and_select_fusion, s32[256]{0:T(256)S(1)} %iota.36), dimensions={0}, to_apply=%region_2.3 | sort | flops 2048 | bytes 4096 | tf_op jit(solution)/shard_map/jit(argsort)/sort | solution.py:45
  4.7 0.6 copy-done.9
  5.3 1.9 gather_fusion
  7.3 0.6 add_select_fusion
  7.9 7.3 %all-to-all-start = ((s32[32,1,8]{2,1,0:T(1,128)}), s32[32,1,8]{2,1,0:T(1,128)S(1)}, u32[]{:S(2)}, u32[]{:S(2)}) async-start(s32[32,1,8]{2,1,0:T(1,128)} %bitcast), calls=%async_computation | async-start | bytes 32768 | tf_op jit(solution)/shard_map/all_to_all | solution.py:48
  15.2 1.5 reshape.152
  16.7 0.3 copy.31
  17.1 5.2 %all-to-all-done = s32[32,1,8]{2,1,0:T(1,128)S(1)} async-done(((s32[32,1,8]{2,1,0:T(1,128)}), s32[32,1,8]{2,1,0:T(1,128)S(1)}, u32[]{:S(2)}, u32[]{:S(2)}) %all-to-all-start) | async-done | bytes 1056 | tf_op jit(solution)/shard_map/all_to_all | solution.py:48
  22.3 1.6 fusion.18
  23.9 2.6 %all-to-all-start.1 = ((f32[32,8,1024]{2,1,0:T(8,128)}), f32[32,8,1024]{2,1,0:T(8,128)S(1)}, u32[]{:S(2)}, u32[]{:S(2)}) async-start(f32[32,8,1024]{2,1,0:T(8,128)} %fusion.18), calls=%async_computation.1 | async-start | bytes 2097152 | tf_op jit(solution)/shard_map/all_to_all | solution.py:58
  26.6 3.2 %sort.32 = (s32[256]{0:T(256)}, s32[256]{0:T(256)S(1)}) sort(s32[256]{0:T(256)S(1)} %get-tuple-element.5, s32[256]{0:T(256)S(1)} %iota.37), dimensions={0}, to_apply=%region_3.4 | sort | flops 2048 | bytes 4096 | tf_op jit(solution)/shard_map/jit(argsort)/sort | solution.py:46
  29.8 0.7 copy.30
  30.6 22.2 %all-to-all-done.1 = f32[32,8,1024]{2,1,0:T(8,128)S(1)} async-done(((f32[32,8,1024]{2,1,0:T(8,128)}), f32[32,8,1024]{2,1,0:T(8,128)S(1)}, u32[]{:S(2)}, u32[]{:S(2)}) %all-to-all-start.1) | async-done | bytes 1048608 | tf_op jit(solution)/shard_map/all_to_all | solution.py:58
  52.8 1.1 gather_fusion.1
  53.9 0.3 copy.33
  54.2 1.3 copy.34
  55.5 4.2 %fusion.12 = f32[256,16,128]{2,1,0:T(8,128)S(1)} fusion(f32[256,16,64]{2,1,0:T(8,128)S(1)} %copy.34, s32[256,128]{1,0:T(8,128)S(1)} %eq.84, f32[256,128]{1,0:T(8,128)S(1)} %mul.64), kind=kOutput, calls=%fused_computation.21 | convolution fusion | flops 405274624 | bytes 3407872 | tf_op jit(solution)/shard_map/bpx,bsx->bps/dot_general | solution.py:66
  59.8 2.0 copy.53
  61.8 1.7 reshape.157
  63.5 0.1 fusion.27
  63.6 1.3 collective-permute-start
  65.0 1.5 collective-permute-start.1
  66.5 3.8 %fusion.11 = f32[32,256,128,1]{2,0,1,3:T(8,128)S(1)} fusion(s32[256,128]{1,0:T(8,128)S(1)} %add_abs_fusion, f32[32,64]{1,0:T(8,128)S(1)} %copy-done.8, f32[32,1]{1,0:T(8,128)S(1)} %copy-done.7), kind=kOutput, calls=%fused_computation.16 | convolution fusion | flops 820021248 | bytes 4333696 | tf_op jit(solution)/shard_map/usk,dk->dus/dot_general | solution.py:93
  70.3 1.2 pad_maximum_fusion.1
  71.5 0.5 copy.48
  72.0 1.2 copy.36
  73.2 0.5 copy.49
  73.7 1.2 copy.37
  74.9 7.9 %fusion.4 = f32[32,128,16,8]{1,2,3,0:T(8,128)S(1)} fusion(f32[16,32,8,128]{3,0,2,1:T(8,128)S(1)} %copy.37, f32[16,32,8,128]{3,0,2,1:T(8,128)S(1)} %copy.36, f32[32,256,128,1]{2,0,1,3:T(8,128)S(1)} %fusion.11), kind=kOutput, calls=%fused_computation.9 | convolution fusion | flops 1611661312 | bytes 10485760 | tf_op jit(solution)/shard_map/pdju,dus->pdjs/dot_general | solution.py:94
  82.8 0.2 bitcast_multiply_fusion
  83.1 6.6 %fusion.1 = f32[256,16,64]{2,1,0:T(8,128)S(1)} fusion(f32[256,16,128]{2,1,0:T(8,128)S(1)} %bitcast_multiply_fusion, s32[256,128]{1,0:T(8,128)S(1)} %eq.84), kind=kOutput, calls=%fused_computation.6 | convolution fusion | flops 404750336 | bytes 3276800 | tf_op jit(solution)/shard_map/bps,bsx->bpx/dot_general | solution.py:98
  89.7 1.0 copy.39
  90.7 0.3 copy.40
  91.1 2.2 %gather_fusion.2 = f32[256,1024]{1,0:T(8,128)} fusion(f32[256,1024]{1,0:T(8,128)S(1)} %copy.40, s32[1024]{0:T(1024)} %copy-done.9), kind=kCustom, calls=%fused_computation.2 | custom fusion | bytes 2098176 | tf_op jit(solution)/shard_map/gather | solution.py:101
  93.3 7.7 %all-to-all-start.2 = ((f32[32,8,1024]{2,1,0:T(8,128)}), f32[32,8,1024]{2,1,0:T(8,128)S(1)}, u32[]{:S(2)}, u32[]{:S(2)}) async-start(f32[32,8,1024]{2,1,0:T(8,128)} %bitcast.17), calls=%async_computation.2 | async-start | bytes 2097152 | tf_op jit(solution)/shard_map/all_to_all | solution.py:102
  100.9 0.5 broadcast.113
  101.5 0.7 reduce.3
  102.2 24.9 %all-to-all-done.2 = f32[32,8,1024]{2,1,0:T(8,128)S(1)} async-done(((f32[32,8,1024]{2,1,0:T(8,128)}), f32[32,8,1024]{2,1,0:T(8,128)S(1)}, u32[]{:S(2)}, u32[]{:S(2)}) %all-to-all-start.2) | async-done | bytes 1048608 | tf_op jit(solution)/shard_map/all_to_all | solution.py:102
  127.2 0.3 copy.41
  127.6 0.7 convolution_bitcast_fusion
  128.2 0.3 copy.42
  128.6 0.4 reshape.164
  129.0 0.3 fusion.14
  129.2 38.5 %all-reduce = (f32[16]{0:T(128)S(1)}, f32[16]{0:T(128)S(1)}) all-reduce(f32[16]{0:T(128)S(1)} %get-tuple-element.17, f32[16]{0:T(128)S(1)} %get-tuple-element.18), channel_id=1, replica_groups=mesh['det'=4,'tm'=8] {'det','tm'}, use_global_device_ids=true, to_apply=%region_1.0 | all-reduce | flops 32 | bytes 256 | tf_op jit(solution)/shard_map/psum | solution.py:42
  167.7 0.3 fusion.13
  168.0 40.8 %psum.23 = f32[16]{0:T(128)S(1)} all-reduce(f32[16]{0:T(128)S(1)} %get-tuple-element.9), channel_id=1, replica_groups=mesh['det'=4,'tm'=8] {'det','tm'}, use_global_device_ids=true, to_apply=%region_7.8 | all-reduce | flops 16 | bytes 128 | tf_op jit(solution)/shard_map/psum | solution.py:118
  208.8 1.1 multiply_add_fusion
  (38 shorter events, 0.4 us)
Async XLA Ops:
  4.7 0.6 copy-start.9
  7.9 14.4 %all-to-all-start = ((s32[32,1,8]{2,1,0:T(1,128)}), s32[32,1,8]{2,1,0:T(1,128)S(1)}, u32[]{:S(2)}, u32[]{:S(2)}) async-start(s32[32,1,8]{2,1,0:T(1,128)} %bitcast), calls=%async_computation | async-start | bytes 32768 | tf_op jit(solution)/shard_map/all_to_all | solution.py:48
  17.0 12.7 %copy-start.10 = (f32[32]{0:T(128)S(1)}, f32[32]{0:T(128)}, u32[]{:S(2)}) copy-start(f32[32]{0:T(128)} %param.16) | copy-start | bytes 388
  17.0 13.4 %copy-start.5 = (s32[32,1024]{1,0:T(8,128)S(1)}, s32[32,1024]{1,0:T(8,128)}, u32[]{:S(2)}) copy-start(s32[32,1024]{1,0:T(8,128)} %param.14) | copy-start | bytes 393220
  17.1 13.4 %copy-start.6 = (f32[32,1024]{1,0:T(8,128)S(1)}, f32[32,1024]{1,0:T(8,128)}, u32[]{:S(2)}) copy-start(f32[32,1024]{1,0:T(8,128)} %param.15) | copy-start | bytes 393220
  23.9 28.9 %all-to-all-start.1 = ((f32[32,8,1024]{2,1,0:T(8,128)}), f32[32,8,1024]{2,1,0:T(8,128)S(1)}, u32[]{:S(2)}, u32[]{:S(2)}) async-start(f32[32,8,1024]{2,1,0:T(8,128)} %fusion.18), calls=%async_computation.1 | async-start | bytes 2097152 | tf_op jit(solution)/shard_map/all_to_all | solution.py:58
  61.8 4.7 %copy-start.7 = (f32[32,1]{1,0:T(8,128)S(1)}, f32[32,1]{1,0:T(8,128)}, u32[]{:S(2)}) copy-start(f32[32,1]{1,0:T(8,128)} %copy.30) | copy-start | bytes 388
  61.8 4.7 %copy-start.8 = (f32[32,64]{1,0:T(8,128)S(1)}, f32[32,64]{1,0:T(8,128)}, u32[]{:S(2)}) copy-start(f32[32,64]{1,0:T(8,128)} %param.17) | copy-start | bytes 24580
  63.6 6.7 %collective-permute-start = (f32[16,32,64]{2,1,0:T(8,128)S(1)}, f32[16,32,64]{2,1,0:T(8,128)S(1)}, u32[]{:S(2)}, u32[]{:S(2)}) collective-permute-start(f32[16,32,64]{2,1,0:T(8,128)S(1)} %get-tuple-element.13), channel_id=1, source_target_pairs={{0,1},{1,2},{2,3},{3,4},{4,5},{5,6},{6,7},{8,9},{9,10},{10,11},{11... | collective-permute-start | bytes 393224 | tf_op jit(solution)/shard_map/ppermute | solution.py:17
  65.0 5.3 %collective-permute-start.1 = (f32[16,32,64]{2,1,0:T(8,128)S(1)}, f32[16,32,64]{2,1,0:T(8,128)S(1)}, u32[]{:S(2)}, u32[]{:S(2)}) collective-permute-start(f32[16,32,64]{2,1,0:T(8,128)S(1)} %get-tuple-element.14), channel_id=1, source_target_pairs={{1,0},{2,1},{3,2},{4,3},{5,4},{6,5},{7,6},{9,8},{10,9},{11,10},{12... | collective-permute-start | bytes 393224 | tf_op jit(solution)/shard_map/ppermute | solution.py:19
  93.3 33.9 %all-to-all-start.2 = ((f32[32,8,1024]{2,1,0:T(8,128)}), f32[32,8,1024]{2,1,0:T(8,128)S(1)}, u32[]{:S(2)}, u32[]{:S(2)}) async-start(f32[32,8,1024]{2,1,0:T(8,128)} %bitcast.17), calls=%async_computation.2 | async-start | bytes 2097152 | tf_op jit(solution)/shard_map/all_to_all | solution.py:102
  127.5 1.4 copy-start
  127.5 1.4 copy-start.2
  127.5 1.4 copy-start.4
  128.6 80.2 %copy-start.3 = (f32[16,8192]{1,0:T(8,128)S(1)}, f32[16,8192]{1,0:T(8,128)}, u32[]{:S(2)}) copy-start(f32[16,8192]{1,0:T(8,128)} %param.9) | copy-start | bytes 1572868
  168.0 41.9 %copy-start.1 = (f32[16,8192]{1,0:T(8,128)}, f32[16,8192]{1,0:T(8,128)S(1)}, u32[]{:S(2)}) copy-start(f32[16,8192]{1,0:T(8,128)S(1)} %get-tuple-element.10) | copy-start | bytes 1572868
where the time goes:
time: 211 us; the launch traced here: 210 us
  blocking collectives  79.3 us (38%)
  waiting for transfers between devices  52.4 us (25%)
  matrix products  24.9 us (12%)
  local copies, waits for them, and re-layouts  21.1 us (10%)
  starting transfers between devices  20.4 us (10%)
  other arithmetic  10.8 us (5%)
    psum x1, blocking collectives, per_device(): norm_new = lax.psum(jnp.sum(new_residual * scaled, axis=1), ('det', 'tm'))  40.8 us
    psum x1, blocking collectives, per_device(): norm_old = lax.psum(local_old, ('det', 'tm'))  38.5 us
    all_to_all x1, waiting for transfers between devices, per_device(): lax.all_to_all(partial_value, ('det', 'tm'), split_axis=0, concat_axis=0,...  24.9 us
    all_to_all x1, waiting for transfers between devices, per_device(): lax.all_to_all(served, ('det', 'tm'), split_axis=0, concat_axis=0, tiled=...  22.2 us
    dot_general x1, matrix products, per_device(): jnp.einsum('pdju,dus->pdjs', windows, toeplitz, precision=lax.Precision.H...  7.91 us
    all_to_all x1, starting transfers between devices, per_device(): lax.all_to_all(partial_value, ('det', 'tm'), split_axis=0, concat_axis=0,...  7.69 us
    all_to_all x1, starting transfers between devices, per_device(): lax.all_to_all(requests, ('det', 'tm'), split_axis=0, concat_axis=0, tile...  7.3 us
    dot_general x1, matrix products, per_device(): jnp.einsum('bps,bsx->bpx', weighted, pixel_hot, precision=lax.Precision.H...  6.59 us
  transfers between devices with their start and end apart: 5, of which 3 were waited for; matrix products, arithmetic and copies ran while one was open for 5% of the time, Pallas kernels for 0%

commit v1 on v0

--- a/solution.py
+++ b/solution.py
@@ -39,7 +39,9 @@
     own_patches = iterate.shape[1] // PX
     width = probes * PX
     local_old = jnp.sum(residual * precond * residual, axis=1)
-    norm_old = lax.psum(local_old, ("det", "tm"))
+    norm_old = local_old
+    for j0 in ("tm", "det"):
+        norm_old = lax.psum(norm_old, j0)
     patch_flat = patch_ids.reshape(blocks)
     owners = patch_flat // own_patches
     sort_order = jnp.argsort(owners, stable=True)

time: 211 us -> 220 us (1.043)
  blocking collectives: 79.3 us -> 105 us
  waiting for transfers between devices: 52.4 us -> 35.9 us
    psum x1 -> x3, blocking collectives: 38.5 us -> 65.3 us  [the longest x1 39.3 us: per_device(): curvature = lax.psum(local_curv, ('det', 'tm'))]
    all_to_all x1, waiting for transfers between devices: 24.9 us -> 8.4 us  [per_device(): lax.all_to_all(partial_value, ('det', 'tm'), split_axis=0, concat_axis=0,...]
where the time goes in v1:
time: 220 us
  blocking collectives  105 us (48%)
  waiting for transfers between devices  35.9 us (16%)
  matrix products  25.5 us (12%)
  local copies, waits for them, and re-layouts  21.1 us (10%)
  starting transfers between devices  19.8 us (9%)
  other arithmetic  11 us (5%)
    psum x1, blocking collectives, per_device(): norm_new = lax.psum(jnp.sum(new_residual * scaled, axis=1), ('det', 'tm'))  40.2 us
    psum x1, blocking collectives, per_device(): curvature = lax.psum(local_curv, ('det', 'tm'))  39.3 us
    psum x2, blocking collectives, per_device(): norm_old = lax.psum(norm_old, j0)  26 us
    all_to_all x1, waiting for transfers between devices, per_device(): lax.all_to_all(served, ('det', 'tm'), split_axis=0, concat_axis=0, tiled=...  22.2 us
    all_to_all x1, waiting for transfers between devices, per_device(): lax.all_to_all(partial_value, ('det', 'tm'), split_axis=0, concat_axis=0,...  8.4 us
    dot_general x1, matrix products, per_device(): jnp.einsum('pdju,dus->pdjs', windows, toeplitz, precision=lax.Precision.H...  7.91 us
    all_to_all x1, starting transfers between devices, per_device(): lax.all_to_all(requests, ('det', 'tm'), split_axis=0, concat_axis=0, tile...  7.3 us
    all_to_all x1, starting transfers between devices, per_device(): lax.all_to_all(partial_value, ('det', 'tm'), split_axis=0, concat_axis=0,...  7.03 us
  transfers between devices with their start and end apart: 5, of which 3 were waited for; matrix products, arithmetic and copies ran while one was open for 5% of the time, Pallas kernels for 0%

profile of v1, /device:TPU:0, one launch (start us, length us, event | category | flops | bytes accessed | tf_op | source)
XLA Modules:
  0.0 219.7 jit_solution(4566914889885449084)
XLA Ops:
  0.6 0.8 copy.28
  1.5 3.2 %sort.31 = (s32[256]{0:T(256)}, s32[256]{0:T(256)S(1)}) sort(s32[256]{0:T(256)S(1)} %and_select_fusion, s32[256]{0:T(256)S(1)} %iota.36), dimensions={0}, to_apply=%region_3.4 | sort | flops 2048 | bytes 4096 | tf_op jit(solution)/shard_map/jit(argsort)/sort | solution.py:47
  4.7 0.6 copy-done.7
  5.3 1.9 gather_fusion
  7.3 0.6 add_select_fusion
  7.9 7.3 %all-to-all-start = ((s32[32,1,8]{2,1,0:T(1,128)}), s32[32,1,8]{2,1,0:T(1,128)S(1)}, u32[]{:S(2)}, u32[]{:S(2)}) async-start(s32[32,1,8]{2,1,0:T(1,128)} %bitcast), calls=%async_computation | async-start | bytes 32768 | tf_op jit(solution)/shard_map/all_to_all | solution.py:50
  15.2 1.5 reshape.152
  16.7 0.3 copy.31
  17.1 5.2 %all-to-all-done = s32[32,1,8]{2,1,0:T(1,128)S(1)} async-done(((s32[32,1,8]{2,1,0:T(1,128)}), s32[32,1,8]{2,1,0:T(1,128)S(1)}, u32[]{:S(2)}, u32[]{:S(2)}) %all-to-all-start) | async-done | bytes 1056 | tf_op jit(solution)/shard_map/all_to_all | solution.py:50
  22.3 1.6 fusion.18
  23.9 2.6 %all-to-all-start.1 = ((f32[32,8,1024]{2,1,0:T(8,128)}), f32[32,8,1024]{2,1,0:T(8,128)S(1)}, u32[]{:S(2)}, u32[]{:S(2)}) async-start(f32[32,8,1024]{2,1,0:T(8,128)} %fusion.18), calls=%async_computation.1 | async-start | bytes 2097152 | tf_op jit(solution)/shard_map/all_to_all | solution.py:60
  26.6 3.2 %sort.32 = (s32[256]{0:T(256)}, s32[256]{0:T(256)S(1)}) sort(s32[256]{0:T(256)S(1)} %get-tuple-element.5, s32[256]{0:T(256)S(1)} %iota.37), dimensions={0}, to_apply=%region_4.5 | sort | flops 2048 | bytes 4096 | tf_op jit(solution)/shard_map/jit(argsort)/sort | solution.py:48
  29.8 0.7 copy.30
  30.6 22.2 %all-to-all-done.1 = f32[32,8,1024]{2,1,0:T(8,128)S(1)} async-done(((f32[32,8,1024]{2,1,0:T(8,128)}), f32[32,8,1024]{2,1,0:T(8,128)S(1)}, u32[]{:S(2)}, u32[]{:S(2)}) %all-to-all-start.1) | async-done | bytes 1048608 | tf_op jit(solution)/shard_map/all_to_all | solution.py:60
  52.8 1.1 gather_fusion.1
  53.9 0.3 copy.33
  54.2 1.3 copy.34
  55.5 4.2 %fusion.12 = f32[256,16,128]{2,1,0:T(8,128)S(1)} fusion(f32[256,16,64]{2,1,0:T(8,128)S(1)} %copy.34, s32[256,128]{1,0:T(8,128)S(1)} %eq.84, f32[256,128]{1,0:T(8,128)S(1)} %mul.64), kind=kOutput, calls=%fused_computation.21 | convolution fusion | flops 405274624 | bytes 3407872 | tf_op jit(solution)/shard_map/bpx,bsx->bps/dot_general | solution.py:68
  59.8 2.0 copy.53
  61.8 1.7 reshape.157
  63.6 1.3 collective-permute-start
  64.9 1.5 collective-permute-start.1
  66.4 4.5 %fusion.11 = f32[32,256,128,1]{2,0,1,3:T(8,128)S(1)} fusion(s32[256,128]{1,0:T(8,128)S(1)} %add_abs_fusion, f32[32,64]{1,0:T(8,128)} %param.17, f32[32,1]{1,0:T(8,128)} %copy.30), kind=kOutput, calls=%fused_computation.16 | convolution fusion | flops 820021248 | bytes 4333696 | tf_op jit(solution)/shard_map/usk,dk->dus/dot_general | solution.py:95
  70.9 1.2 pad_maximum_fusion.1
  72.2 0.5 copy.48
  72.6 1.2 copy.36
  73.9 0.5 copy.49
  74.3 1.2 copy.37
  75.6 7.9 %fusion.4 = f32[32,128,16,8]{1,2,3,0:T(8,128)S(1)} fusion(f32[16,32,8,128]{3,0,2,1:T(8,128)S(1)} %copy.37, f32[16,32,8,128]{3,0,2,1:T(8,128)S(1)} %copy.36, f32[32,256,128,1]{2,0,1,3:T(8,128)S(1)} %fusion.11), kind=kOutput, calls=%fused_computation.9 | convolution fusion | flops 1611661312 | bytes 10485760 | tf_op jit(solution)/shard_map/pdju,dus->pdjs/dot_general | solution.py:96
  83.5 0.2 bitcast_multiply_fusion
  83.7 6.6 %fusion.1 = f32[256,16,64]{2,1,0:T(8,128)S(1)} fusion(f32[256,16,128]{2,1,0:T(8,128)S(1)} %bitcast_multiply_fusion, s32[256,128]{1,0:T(8,128)S(1)} %eq.84), kind=kOutput, calls=%fused_computation.6 | convolution fusion | flops 404750336 | bytes 3276800 | tf_op jit(solution)/shard_map/bps,bsx->bpx/dot_general | solution.py:100
  90.3 1.0 copy.39
  91.4 0.3 copy.40
  91.7 2.2 gather_fusion.2
  93.9 7.0 %all-to-all-start.2 = ((f32[32,8,1024]{2,1,0:T(8,128)}), f32[32,8,1024]{2,1,0:T(8,128)S(1)}, u32[]{:S(2)}, u32[]{:S(2)}) async-start(f32[32,8,1024]{2,1,0:T(8,128)} %bitcast.17), calls=%async_computation.2 | async-start | bytes 2097152 | tf_op jit(solution)/shard_map/all_to_all | solution.py:104
  101.2 16.3 %psum.28 = f32[16]{0:T(128)S(1)} all-reduce(f32[16]{0:T(128)S(1)} %fusion.14), channel_id=1, replica_groups=mesh['det'=4,'tm'=8] {'tm'}, use_global_device_ids=true, to_apply=%region_1.0 | all-reduce | flops 16 | bytes 128 | tf_op jit(solution)/shard_map/psum | solution.py:44
  117.5 0.5 broadcast.113
  118.0 0.7 reduce.3
  118.8 8.4 %all-to-all-done.2 = f32[32,8,1024]{2,1,0:T(8,128)S(1)} async-done(((f32[32,8,1024]{2,1,0:T(8,128)}), f32[32,8,1024]{2,1,0:T(8,128)S(1)}, u32[]{:S(2)}, u32[]{:S(2)}) %all-to-all-start.2) | async-done | bytes 1048608 | tf_op jit(solution)/shard_map/all_to_all | solution.py:104
  127.2 0.3 copy.41
  127.5 0.7 convolution_bitcast_fusion
  128.2 0.3 copy.42
  128.5 0.4 reshape.164
  129.1 9.7 %psum.29 = f32[16]{0:T(128)S(1)} all-reduce(f32[16]{0:T(128)S(1)} %psum.28), channel_id=1, replica_groups=mesh['det'=4,'tm'=8] {'det'}, use_global_device_ids=true, to_apply=%region_2.0 | all-reduce | flops 16 | bytes 128 | tf_op jit(solution)/shard_map/psum | solution.py:44
  138.8 39.3 %psum.30 = f32[16]{0:T(128)S(1)} all-reduce(f32[16]{0:T(128)S(1)} %multiply_reduce_fusion), channel_id=1, replica_groups=mesh['det'=4,'tm'=8] {'det','tm'}, use_global_device_ids=true, to_apply=%region_6.7 | all-reduce | flops 16 | bytes 128 | tf_op jit(solution)/shard_map/psum | solution.py:115
  178.1 0.3 fusion.13
  178.4 40.2 %psum.31 = f32[16]{0:T(128)S(1)} all-reduce(f32[16]{0:T(128)S(1)} %get-tuple-element.7), channel_id=1, replica_groups=mesh['det'=4,'tm'=8] {'det','tm'}, use_global_device_ids=true, to_apply=%region_8.9 | all-reduce | flops 16 | bytes 128 | tf_op jit(solution)/shard_map/psum | solution.py:120
  218.6 1.1 multiply_add_fusion
  (37 shorter events, 1.0 us)
Async XLA Ops:
  4.7 0.6 copy-start.7
  7.9 14.4 %all-to-all-start = ((s32[32,1,8]{2,1,0:T(1,128)}), s32[32,1,8]{2,1,0:T(1,128)S(1)}, u32[]{:S(2)}, u32[]{:S(2)}) async-start(s32[32,1,8]{2,1,0:T(1,128)} %bitcast), calls=%async_computation | async-start | bytes 32768 | tf_op jit(solution)/shard_map/all_to_all | solution.py:50
  17.0 12.7 %copy-start.8 = (f32[32]{0:T(128)S(1)}, f32[32]{0:T(128)}, u32[]{:S(2)}) copy-start(f32[32]{0:T(128)} %param.16) | copy-start | bytes 388
  17.0 13.4 %copy-start.5 = (s32[32,1024]{1,0:T(8,128)S(1)}, s32[32,1024]{1,0:T(8,128)}, u32[]{:S(2)}) copy-start(s32[32,1024]{1,0:T(8,128)} %param.14) | copy-start | bytes 393220
  17.1 13.4 %copy-start.6 = (f32[32,1024]{1,0:T(8,128)S(1)}, f32[32,1024]{1,0:T(8,128)}, u32[]{:S(2)}) copy-start(f32[32,1024]{1,0:T(8,128)} %param.15) | copy-start | bytes 393220
  23.9 28.9 %all-to-all-start.1 = ((f32[32,8,1024]{2,1,0:T(8,128)}), f32[32,8,1024]{2,1,0:T(8,128)S(1)}, u32[]{:S(2)}, u32[]{:S(2)}) async-start(f32[32,8,1024]{2,1,0:T(8,128)} %fusion.18), calls=%async_computation.1 | async-start | bytes 2097152 | tf_op jit(solution)/shard_map/all_to_all | solution.py:60
  63.6 7.3 %collective-permute-start = (f32[16,32,64]{2,1,0:T(8,128)S(1)}, f32[16,32,64]{2,1,0:T(8,128)S(1)}, u32[]{:S(2)}, u32[]{:S(2)}) collective-permute-start(f32[16,32,64]{2,1,0:T(8,128)S(1)} %get-tuple-element.11), channel_id=1, source_target_pairs={{0,1},{1,2},{2,3},{3,4},{4,5},{5,6},{6,7},{8,9},{9,10},{10,11},{11... | collective-permute-start | bytes 393224 | tf_op jit(solution)/shard_map/ppermute | solution.py:17
  64.9 6.0 %collective-permute-start.1 = (f32[16,32,64]{2,1,0:T(8,128)S(1)}, f32[16,32,64]{2,1,0:T(8,128)S(1)}, u32[]{:S(2)}, u32[]{:S(2)}) collective-permute-start(f32[16,32,64]{2,1,0:T(8,128)S(1)} %get-tuple-element.12), channel_id=1, source_target_pairs={{1,0},{2,1},{3,2},{4,3},{5,4},{6,5},{7,6},{9,8},{10,9},{11,10},{12... | collective-permute-start | bytes 393224 | tf_op jit(solution)/shard_map/ppermute | solution.py:19
  93.9 7.0 %copy-start.1 = (f32[16,8192]{1,0:T(8,128)S(1)}, f32[16,8192]{1,0:T(8,128)}, u32[]{:S(2)}) copy-start(f32[16,8192]{1,0:T(8,128)} %param.10) | copy-start | bytes 1572868
  93.9 7.1 %copy-start.4 = (f32[8192]{0:T(1024)S(1)}, f32[8192]{0:T(1024)}, u32[]{:S(2)}) copy-start(f32[8192]{0:T(1024)} %param.12) | copy-start | bytes 98308
  93.9 33.3 %all-to-all-start.2 = ((f32[32,8,1024]{2,1,0:T(8,128)}), f32[32,8,1024]{2,1,0:T(8,128)S(1)}, u32[]{:S(2)}, u32[]{:S(2)}) async-start(f32[32,8,1024]{2,1,0:T(8,128)} %bitcast.17), calls=%async_computation.2 | async-start | bytes 2097152 | tf_op jit(solution)/shard_map/all_to_all | solution.py:104
  127.5 1.4 copy-start
  128.5 90.1 %copy-start.3 = (f32[16,8192]{1,0:T(8,128)S(1)}, f32[16,8192]{1,0:T(8,128)}, u32[]{:S(2)}) copy-start(f32[16,8192]{1,0:T(8,128)} %param.9) | copy-start | bytes 1572868
  178.4 41.3 %copy-start.2 = (f32[16,8192]{1,0:T(8,128)}, f32[16,8192]{1,0:T(8,128)S(1)}, u32[]{:S(2)}) copy-start(f32[16,8192]{1,0:T(8,128)S(1)} %get-tuple-element.8) | copy-start | bytes 1572868
